TPU v7x, 32 devices: a whole 2x2x4 slice. The times are simulated.
32 devices in a mesh: vox: 8 (over y, x, core), tm: 4 (over z).
Axes of the slice: x: 2, y: 2, z: 4, core: 2. Of those that a mesh axis runs over, the one named last changes fastest.
Arguments:
- series: float32 [2048, 16384], P('tm', 'vox'), may hold values from -40 to 40
- spikes: int32 [2048, 16384], P('tm', 'vox'), may hold values from 0 to 15
- motion: float32 [2048, 6], P('tm'), may hold values from -5 to 5
- tissue: float32 [3, 16384], P(None, 'vox'), may hold values from 0.01 to 12, as said below
Outputs:
- cleaned: float32 [2048, 16384], P('tm', 'vox')
Inputs may be any that keep to these rules, and one draw needn't show every extreme that they name: Bit j-1 of an entry (spikes // 2^(j-1) odd) flags that frame's level-j coefficient of that voxel as a spike. `tissue`: all weights are positive.
All inputs are finite; a program needn't handle non-finite values.
Results may differ from a plain program's by a relative error of at most 0.0003.
Values sent between devices are 32-bit elements; how exact they have to be, the bound alone decides.
A program may use at most 64 MiB of HBM per device.

v0:
```python
import jax
import jax.numpy as jnp
from jax import lax
from jax.sharding import PartitionSpec as P

LEVELS = 4


def from_behind(block, axis, distance):
    devices = range(lax.axis_size(axis))
    route = [((i - distance) % len(devices), i) for i in devices]
    return lax.ppermute(block, axis, route)


def shifted(block, axis, distance):
    devices = range(lax.axis_size(axis))
    route = [(i - distance, i) for i in devices if i - distance in devices]
    return lax.ppermute(block, axis, route)


def precise_product(left, right):
    return jnp.dot(left, right, precision=lax.Precision.HIGHEST, preferred_element_type=jnp.float32)


def keep_level(spikes, level):
    return 1.0 - (spikes // 2**level % 2).astype(jnp.float32)


def despike_levelwise(series, spikes):
    frames = series.shape[0]
    approx = series
    kept_list = []
    for level in range(LEVELS):
        shift_rows = 2**level
        earlier = from_behind(approx[frames - shift_rows :], "tm", 1)
        lagged = jnp.concatenate([earlier, approx[: frames - shift_rows]], axis=0)
        detail = (approx - lagged) * 0.5
        kept_list.append(detail * keep_level(spikes, level))
        approx = (approx + lagged) * 0.5
    for level in range(LEVELS - 1, -1, -1):
        shift_rows = 2**level
        kept = kept_list[level]
        heads = from_behind(jnp.stack([approx[:shift_rows], kept[:shift_rows]]), "tm", -1)
        lead_approx = jnp.concatenate([approx[shift_rows:], heads[0]], axis=0)
        lead_kept = jnp.concatenate([kept[shift_rows:], heads[1]], axis=0)
        approx = (approx + lead_approx) * 0.5 + (kept - lead_kept) * 0.5
    return approx


def local(series, spikes, motion, tissue):
    spike_free_series = despike_levelwise(series, spikes)
    numer = precise_product(spike_free_series, tissue.T)
    numer = lax.psum(numer, "vox")
    voxel_signals = numer / float(tissue.shape[1] * lax.axis_size("vox"))
    base_regressors = jnp.concatenate([motion, voxel_signals], axis=1)
    previous_frames = shifted(base_regressors[base_regressors.shape[0] - 1 :], "tm", 1)
    before = jnp.concatenate([previous_frames, base_regressors[:-1]], axis=0)
    temporal_derivative = base_regressors - before
    nuisance_matrix = jnp.concatenate(
        [
            base_regressors,
            temporal_derivative,
            base_regressors * base_regressors,
            temporal_derivative * temporal_derivative,
        ],
        axis=1,
    )
    gram_matrix = precise_product(nuisance_matrix.T, nuisance_matrix)
    cross_products = precise_product(nuisance_matrix.T, spike_free_series)
    gram_matrix, cross_products = lax.psum((gram_matrix, cross_products), "tm")
    factor = jnp.linalg.cholesky(gram_matrix)
    beta_estimates = jax.scipy.linalg.cho_solve((factor, True), cross_products)
    return spike_free_series - precise_product(nuisance_matrix, beta_estimates)


def solution(mesh):
    return jax.shard_map(
        local,
        mesh=mesh,
        in_specs=(P("tm", "vox"), P("tm", "vox"), P("tm", None), P(None, "vox")),
        out_specs=P("tm", "vox"),
        check_vma=False,
    )
```

profile of v0, /device:TPU:0, one launch (start us, length us, event | category | flops | bytes accessed | tf_op | source)
XLA Modules:
  0.0 185.3 jit_solution(8854864835814602594)
XLA Ops:
  6.5 0.9 slice.120
  7.4 3.0 %collective-permute-start = (f32[1,2048]{1,0:T(1,128)S(1)}, f32[1,2048]{1,0:T(1,128)S(1)}, u32[]{:S(2)}, u32[]{:S(2)}) collective-permute-start(f32[1,2048]{1,0:T(1,128)S(1)} %slice.120), channel_id=1, source_target_pairs={{3,0},{0,1},{1,2},{2,3},{7,4},{4,5},{5,6},{6,7},{11,8},{8,9},{9,10... | collective-permute-start | bytes 24584 | tf_op jit(solution)/shard_map/ppermute | solution.py:12
  10.4 3.7 %collective-permute-done = f32[1,2048]{1,0:T(1,128)S(1)} collective-permute-done((f32[1,2048]{1,0:T(1,128)S(1)}, f32[1,2048]{1,0:T(1,128)S(1)}, u32[]{:S(2)}, u32[]{:S(2)}) %collective-permute-start) | collective-permute-done | bytes 8224 | tf_op jit(solution)/shard_map/ppermute | solution.py:12
  14.1 6.2 %fusion.16 = (f32[512,2048]{1,0:T(8,128)S(1)}, f32[512,2048]{1,0:T(8,128)S(1)}) fusion(f32[512,2048]{1,0:T(8,128)} %param.4, f32[511,2048]{1,0:T(8,128)} %bitcast.58, f32[1,2048]{1,0:T(1,128)S(1)} %collective-permute-done, s32[512,2048]{1,0:T(8,128)} %param.5), kind=kLoop, calls=%fused_computation.36 | loop fusion | flops 19922944 | bytes 20971520 | tf_op jit(solution)/shard_map/mul | solution.py:38
  20.4 5.5 %collective-permute-done.1 = f32[2,2048]{1,0:T(2,128)S(1)} collective-permute-done((f32[2,2048]{1,0:T(2,128)S(1)}, f32[2,2048]{1,0:T(2,128)S(1)}, u32[]{:S(2)}, u32[]{:S(2)}) %collective-permute-start.1) | collective-permute-done | bytes 16416 | tf_op jit(solution)/shard_map/ppermute | solution.py:12
  25.9 5.1 %fusion.13 = (f32[512,2048]{1,0:T(8,128)S(1)}, f32[512,2048]{1,0:T(8,128)S(1)}) fusion(f32[512,2048]{1,0:T(8,128)S(1)} %get-tuple-element.12, f32[510,2048]{1,0:T(8,128)S(1)} %bitcast.57, f32[2,2048]{1,0:T(2,128)S(1)} %collective-permute-done.1, s32[512,2048]{1,0:T(8,128)S(1)} %copy-done.1), kind=kLoop, calls=%fused_computation.33 | loop fusion | flops 35651584 | bytes 20971520 | tf_op jit(solution)/shard_map/mul | solution.py:38
  31.0 5.7 %collective-permute-done.2 = f32[4,2048]{1,0:T(4,128)S(1)} collective-permute-done((f32[4,2048]{1,0:T(4,128)S(1)}, f32[4,2048]{1,0:T(4,128)S(1)}, u32[]{:S(2)}, u32[]{:S(2)}) %collective-permute-start.2) | collective-permute-done | bytes 32800 | tf_op jit(solution)/shard_map/ppermute | solution.py:12
  36.7 5.1 %fusion.9 = (f32[512,2048]{1,0:T(8,128)S(1)}, f32[512,2048]{1,0:T(8,128)S(1)}) fusion(f32[512,2048]{1,0:T(8,128)S(1)} %get-tuple-element.10, f32[508,2048]{1,0:T(8,128)S(1)} %bitcast.56, f32[4,2048]{1,0:T(4,128)S(1)} %collective-permute-done.2, s32[512,2048]{1,0:T(8,128)S(1)} %copy-done.1), kind=kLoop, calls=%fused_computation.29 | loop fusion | flops 35651584 | bytes 20971520 | tf_op jit(solution)/shard_map/mul | solution.py:38
  42.4 5.6 %collective-permute-done.3 = f32[8,2048]{1,0:T(8,128)S(1)} collective-permute-done((f32[8,2048]{1,0:T(8,128)S(1)}, f32[8,2048]{1,0:T(8,128)S(1)}, u32[]{:S(2)}, u32[]{:S(2)}) %collective-permute-start.3) | collective-permute-done | bytes 65568 | tf_op jit(solution)/shard_map/ppermute | solution.py:12
  48.0 4.8 %fusion.4 = (f32[512,2048]{1,0:T(8,128)S(1)}, f32[512,2048]{1,0:T(8,128)S(1)}) fusion(f32[512,2048]{1,0:T(8,128)S(1)} %get-tuple-element.8, f32[504,2048]{1,0:T(8,128)S(1)} %slice.159, f32[8,2048]{1,0:T(8,128)S(1)} %collective-permute-done.3, s32[512,2048]{1,0:T(8,128)S(1)} %copy-done.1), kind=kLoop, calls=%fused_computation.24 | loop fusion | flops 35651584 | bytes 20971520 | tf_op jit(solution)/shard_map/mul | solution.py:38
  53.9 4.5 %collective-permute-done.4 = f32[2,8,2048]{2,1,0:T(8,128)S(1)} collective-permute-done((f32[2,8,2048]{2,1,0:T(8,128)S(1)}, f32[2,8,2048]{2,1,0:T(8,128)S(1)}, u32[]{:S(2)}, u32[]{:S(2)}) %collective-permute-start.4) | collective-permute-done | bytes 131104 | tf_op jit(solution)/shard_map/ppermute | solution.py:12
  58.4 2.4 %fusion.18 = f32[512,2048]{1,0:T(8,128)S(1)} fusion(f32[512,2048]{1,0:T(8,128)S(1)} %get-tuple-element.14, f32[8,2048]{1,0:T(8,128)S(1)} %get-tuple-element.16, f32[504,2048]{1,0:T(8,128)S(1)} %slice.160, f32[512,2048]{1,0:T(8,128)S(1)} %get-tuple-element.13, f32[8,2048]{1,0:T(8,128)S(1)} %get-tuple-element.15, f32[504,2048]{1,0:T(8,128)S(1)} %slice.164), kind=kLoop, calls=%fused_computation.43 | loop fusion | flops 6291456 | bytes 20971520 | tf_op jit(solution)/shard_map/add | solution.py:46
  60.8 1.3 collective-permute-start.5
  62.9 0.7 slice.166
  63.6 1.5 collective-permute-done.5
  65.1 2.4 %fusion.20 = f32[512,2048]{1,0:T(8,128)S(1)} fusion(f32[512,2048]{1,0:T(8,128)S(1)} %fusion.18, f32[4,2048]{1,0:T(4,128)S(1)} %get-tuple-element.18, f32[508,2048]{1,0:T(8,128)S(1)} %slice.166, f32[512,2048]{1,0:T(8,128)S(1)} %get-tuple-element.7, f32[4,2048]{1,0:T(4,128)S(1)} %get-tuple-element.17, f32[508,2048]{1,0:T(8,128)S(1)} %slice.170), kind=kLoop, calls=%fused_computation.47 | loop fusion | flops 6291456 | bytes 20971520 | tf_op jit(solution)/shard_map/add | solution.py:46
  67.6 3.3 %collective-permute-start.6 = (f32[2,2,2048]{2,1,0:T(2,128)S(1)}, f32[2,2,2048]{2,1,0:T(2,128)S(1)}, u32[]{:S(2)}, u32[]{:S(2)}) collective-permute-start(f32[2,2,2048]{2,1,0:T(2,128)S(1)} %pad_maximum_fusion.7), channel_id=1, source_target_pairs={{1,0},{2,1},{3,2},{0,3},{5,4},{6,5},{7,6},{4,7},{9,8},{10,9},{11,1... | collective-permute-start | bytes 98312 | tf_op jit(solution)/shard_map/ppermute | solution.py:12
  72.5 2.4 %fusion.22 = f32[512,2048]{1,0:T(8,128)S(1)} fusion(f32[512,2048]{1,0:T(8,128)S(1)} %fusion.20, f32[2,2048]{1,0:T(2,128)S(1)} %get-tuple-element.20, f32[510,2048]{1,0:T(8,128)S(1)} %slice.172, f32[512,2048]{1,0:T(8,128)S(1)} %get-tuple-element.9, f32[2,2048]{1,0:T(2,128)S(1)} %get-tuple-element.19, f32[510,2048]{1,0:T(8,128)S(1)} %slice.176), kind=kLoop, calls=%fused_computation.51 | loop fusion | flops 6291456 | bytes 20971520 | tf_op jit(solution)/shard_map/add | solution.py:46
  75.0 4.2 %collective-permute-start.7 = (f32[2,1,2048]{2,1,0:T(1,128)S(1)}, f32[2,1,2048]{2,1,0:T(1,128)S(1)}, u32[]{:S(2)}, u32[]{:S(2)}) collective-permute-start(f32[2,1,2048]{2,1,0:T(1,128)S(1)} %pad_maximum_fusion.8), channel_id=1, source_target_pairs={{1,0},{2,1},{3,2},{0,3},{5,4},{6,5},{7,6},{4,7},{9,8},{10,9},{11,1... | collective-permute-start | bytes 49160 | tf_op jit(solution)/shard_map/ppermute | solution.py:12
  80.7 2.5 %fusion.24 = f32[512,2048]{1,0:T(8,128)S(1)} fusion(f32[512,2048]{1,0:T(8,128)S(1)} %fusion.22, f32[1,2048]{1,0:T(1,128)S(1)} %get-tuple-element.23, f32[511,2048]{1,0:T(8,128)S(1)} %slice.178, f32[512,2048]{1,0:T(8,128)S(1)} %get-tuple-element.11, f32[1,2048]{1,0:T(1,128)S(1)} %get-tuple-element.22, f32[511,2048]{1,0:T(8,128)S(1)} %slice.182), kind=kLoop, calls=%fused_computation.55 | loop fusion | flops 6291456 | bytes 20971520 | tf_op jit(solution)/shard_map/add | solution.py:46
  83.2 2.0 %copy-done.2 = f32[512,2048]{1,0:T(8,128)} copy-done((f32[512,2048]{1,0:T(8,128)}, f32[512,2048]{1,0:T(8,128)S(1)}, u32[]{:S(2)}) %copy-start.2) | copy-done | bytes 4194328
  85.2 3.6 %fusion.38 = f32[512,3]{0,1:T(4,128)S(1)} fusion(f32[512,2048]{1,0:T(8,128)S(1)} %fusion.24, f32[3,2048]{1,0:T(4,128)S(1)} %copy-done), kind=kOutput, calls=%fused_computation.109 | convolution fusion | flops 37748736 | bytes 4225024 | tf_op jit(solution)/shard_map/dot_general | solution.py:22
  88.8 12.0 %psum.21 = f32[512,3]{0,1:T(4,128)S(1)} all-reduce(f32[512,3]{0,1:T(4,128)S(1)} %fusion.38), channel_id=1, replica_groups=mesh['vox'=8,'tm'=4] {'vox'}, use_global_device_ids=true, to_apply=%region_0.1 | all-reduce | flops 1536 | bytes 12288 | tf_op jit(solution)/shard_map/psum | solution.py:53
  101.0 1.3 collective-permute-start.8
  102.2 1.3 collective-permute-done.8
  104.4 5.4 %fusion.40 = f32[36,2048]{1,0:T(8,128)} fusion(f32[512,36]{0,1:T(8,128)S(1)} %concatenate.60, f32[512,2048]{1,0:T(8,128)} %copy-done.2), kind=kOutput, calls=%fused_computation.111 | convolution fusion | flops 452984832 | bytes 4562944 | tf_op jit(solution)/shard_map/dot_general | solution.py:22
  109.8 22.6 %psum.22 = f32[36,36]{0,1:T(8,128)S(1)} all-reduce(f32[36,36]{0,1:T(8,128)S(1)} %fusion.39), channel_id=1, replica_groups=mesh['vox'=8,'tm'=4] {'tm'}, use_global_device_ids=true, to_apply=%region_1.2 | all-reduce | flops 1296 | bytes 10368 | tf_op jit(solution)/shard_map/psum | solution.py:70
  132.5 3.3 %cholesky.16 = f32[36,36]{1,0:T(8,128)S(1)} custom-call(f32[36,36]{1,0:T(8,128)S(1)} %fusion.35), custom_call_target="Cholesky" | custom-call | tf_op jit(solution)/shard_map/jit(cholesky)/cholesky | solution.py:71
  137.1 2.8 %custom-call.10 = f32[1,36,36]{1,2,0:T(8,128)S(1)} custom-call(f32[1,36,36]{2,1,0:T(8,128)S(1)} %fusion.30), custom_call_target="InvertDiagBlocksLowerTriangular" | custom-call | tf_op jit(solution)/shard_map/jit(_cho_solve)/triangular_solve | solution.py:72
  139.9 30.1 %all-reduce.2.cloned.1.call-done = f32[36,2048]{1,0:T(8,128)} async-done(((f32[36,2048]{1,0:T(8,128)}), f32[36,2048]{1,0:T(8,128)}) %all-reduce.2.cloned.1.call-update) | async-done | bytes 294928 | tf_op jit(solution)/shard_map/psum | solution.py:70
  170.0 1.4 fusion.33
  171.8 6.6 %convolution_subtract_fusion = f32[512,2048]{1,0:T(8,128)} fusion(f32[512,2048]{1,0:T(8,128)} %copy-done.2, f32[512,36]{0,1:T(8,128)S(1)} %concatenate.60, f32[36,2048]{1,0:T(8,128)S(1)} %fusion.31), kind=kOutput, calls=%fused_computation.64 | convolution fusion | flops 454033408 | bytes 8757248 | tf_op jit(solution)/shard_map/dot_general | solution.py:22
  (53 shorter events, 8.3 us)
Async XLA Ops:
  6.5 78.6 %copy-start = (f32[3,2048]{1,0:T(4,128)S(1)}, f32[3,2048]{1,0:T(4,128)}, u32[]{:S(2)}) copy-start(f32[3,2048]{1,0:T(4,128)} %param.7) | copy-start | bytes 73732
  6.5 163.4 %all-reduce.2.cloned.1.call-start = ((), (), s32[]{:S(2)}) async-start(), calls=%async_computation | async-start | bytes 655360 | tf_op jit(solution)/shard_map/psum | solution.py:70
  7.4 6.7 %collective-permute-start = (f32[1,2048]{1,0:T(1,128)S(1)}, f32[1,2048]{1,0:T(1,128)S(1)}, u32[]{:S(2)}, u32[]{:S(2)}) collective-permute-start(f32[1,2048]{1,0:T(1,128)S(1)} %slice.120), channel_id=1, source_target_pairs={{3,0},{0,1},{1,2},{2,3},{7,4},{4,5},{5,6},{6,7},{11,8},{8,9},{9,10... | collective-permute-start | bytes 24584 | tf_op jit(solution)/shard_map/ppermute | solution.py:12
  14.1 11.8 %copy-start.1 = (s32[512,2048]{1,0:T(8,128)S(1)}, s32[512,2048]{1,0:T(8,128)}, u32[]{:S(2)}) copy-start(s32[512,2048]{1,0:T(8,128)} %param.5) | copy-start | bytes 12582916
  20.3 5.6 %collective-permute-start.1 = (f32[2,2048]{1,0:T(2,128)S(1)}, f32[2,2048]{1,0:T(2,128)S(1)}, u32[]{:S(2)}, u32[]{:S(2)}) collective-permute-start(f32[2,2048]{1,0:T(2,128)S(1)} %slice.154), channel_id=1, source_target_pairs={{3,0},{0,1},{1,2},{2,3},{7,4},{4,5},{5,6},{6,7},{11,8},{8,9},{9,10... | collective-permute-start | bytes 49160 | tf_op jit(solution)/shard_map/ppermute | solution.py:12
  31.0 5.8 %collective-permute-start.2 = (f32[4,2048]{1,0:T(4,128)S(1)}, f32[4,2048]{1,0:T(4,128)S(1)}, u32[]{:S(2)}, u32[]{:S(2)}) collective-permute-start(f32[4,2048]{1,0:T(4,128)S(1)} %slice.156), channel_id=1, source_target_pairs={{3,0},{0,1},{1,2},{2,3},{7,4},{4,5},{5,6},{6,7},{11,8},{8,9},{9,10... | collective-permute-start | bytes 98312 | tf_op jit(solution)/shard_map/ppermute | solution.py:12
  41.8 6.1 %collective-permute-start.3 = (f32[8,2048]{1,0:T(8,128)S(1)}, f32[8,2048]{1,0:T(8,128)S(1)}, u32[]{:S(2)}, u32[]{:S(2)}) collective-permute-start(f32[8,2048]{1,0:T(8,128)S(1)} %slice.158), channel_id=1, source_target_pairs={{3,0},{0,1},{1,2},{2,3},{7,4},{4,5},{5,6},{6,7},{11,8},{8,9},{9,10... | collective-permute-start | bytes 196616 | tf_op jit(solution)/shard_map/ppermute | solution.py:12
  52.8 5.6 %collective-permute-start.4 = (f32[2,8,2048]{2,1,0:T(8,128)S(1)}, f32[2,8,2048]{2,1,0:T(8,128)S(1)}, u32[]{:S(2)}, u32[]{:S(2)}) collective-permute-start(f32[2,8,2048]{2,1,0:T(8,128)S(1)} %pad_maximum_fusion.4), channel_id=1, source_target_pairs={{1,0},{2,1},{3,2},{0,3},{5,4},{6,5},{7,6},{4,7},{9,8},{10,9},{11,1... | collective-permute-start | bytes 393224 | tf_op jit(solution)/shard_map/ppermute | solution.py:12
  60.8 4.3 %collective-permute-start.5 = (f32[2,4,2048]{2,1,0:T(4,128)S(1)}, f32[2,4,2048]{2,1,0:T(4,128)S(1)}, u32[]{:S(2)}, u32[]{:S(2)}) collective-permute-start(f32[2,4,2048]{2,1,0:T(4,128)S(1)} %pad_maximum_fusion.5), channel_id=1, source_target_pairs={{1,0},{2,1},{3,2},{0,3},{5,4},{6,5},{7,6},{4,7},{9,8},{10,9},{11,1... | collective-permute-start | bytes 196616 | tf_op jit(solution)/shard_map/ppermute | solution.py:12
  67.6 4.9 %collective-permute-start.6 = (f32[2,2,2048]{2,1,0:T(2,128)S(1)}, f32[2,2,2048]{2,1,0:T(2,128)S(1)}, u32[]{:S(2)}, u32[]{:S(2)}) collective-permute-start(f32[2,2,2048]{2,1,0:T(2,128)S(1)} %pad_maximum_fusion.7), channel_id=1, source_target_pairs={{1,0},{2,1},{3,2},{0,3},{5,4},{6,5},{7,6},{4,7},{9,8},{10,9},{11,1... | collective-permute-start | bytes 98312 | tf_op jit(solution)/shard_map/ppermute | solution.py:12
  75.0 5.6 %collective-permute-start.7 = (f32[2,1,2048]{2,1,0:T(1,128)S(1)}, f32[2,1,2048]{2,1,0:T(1,128)S(1)}, u32[]{:S(2)}, u32[]{:S(2)}) collective-permute-start(f32[2,1,2048]{2,1,0:T(1,128)S(1)} %pad_maximum_fusion.8), channel_id=1, source_target_pairs={{1,0},{2,1},{3,2},{0,3},{5,4},{6,5},{7,6},{4,7},{9,8},{10,9},{11,1... | collective-permute-start | bytes 49160 | tf_op jit(solution)/shard_map/ppermute | solution.py:12
  83.1 2.0 %copy-start.2 = (f32[512,2048]{1,0:T(8,128)}, f32[512,2048]{1,0:T(8,128)S(1)}, u32[]{:S(2)}) copy-start(f32[512,2048]{1,0:T(8,128)S(1)} %fusion.24) | copy-start | bytes 12582916
  85.2 15.7 %copy-start.3 = (f32[512,6]{0,1:T(8,128)S(1)}, f32[512,6]{0,1:T(8,128)}, u32[]{:S(2)}) copy-start(f32[512,6]{0,1:T(8,128)} %param.6) | copy-start | bytes 36868
  101.0 2.6 %collective-permute-start.8 = (f32[1,9]{0,1:T(8,128)S(1)}, f32[1,9]{0,1:T(8,128)S(1)}, u32[]{:S(2)}, u32[]{:S(2)}) collective-permute-start(f32[1,9]{0,1:T(8,128)S(1)} %fusion.36), channel_id=1, source_target_pairs={{0,1},{1,2},{2,3},{4,5},{5,6},{6,7},{8,9},{9,10},{10,11},{12,13},{... | collective-permute-start | bytes 116 | tf_op jit(solution)/shard_map/ppermute | solution.py:18
Sparse Core Ops, SparseCore 0:
  136.0 33.9 all-reduce.1
where the time goes:
time: 186 us; the launch traced here: 185 us
  waiting for transfers between devices  58.1 us (31%)
  other arithmetic  38.5 us (21%)
  blocking collectives  34.6 us (19%)
  matrix products  17.8 us (10%)
  between operations  13.8 us (7%)
  starting transfers between devices  13.3 us (7%)
  local copies, waits for them, and re-layouts  9.3 us (5%)
    psum x1, waiting for transfers between devices, local(): gram_matrix, cross_products = lax.psum((gram_matrix, cross_products), 'tm')  30.1 us
    ppermute x8, waiting for transfers between devices, from_behind(): return lax.ppermute(block, axis, route)  26.6 us
    psum x1, blocking collectives, local(): gram_matrix, cross_products = lax.psum((gram_matrix, cross_products), 'tm')  22.6 us
    mul x4, other arithmetic, despike_levelwise(): kept_list.append(detail * keep_level(spikes, level))  21.1 us
    dot_general x4, matrix products, precise_product(): jnp.dot(left, right, precision=lax.Precision.HIGHEST, preferred_element_t...  15.9 us
    ppermute x8, starting transfers between devices, from_behind(): return lax.ppermute(block, axis, route)  12 us
    psum x1, blocking collectives, local(): numer = lax.psum(numer, 'vox')  12 us
    add x4, other arithmetic, despike_levelwise(): approx = (approx + lead_approx) * 0.5 + (kept - lead_kept) * 0.5  9.76 us
  transfers between devices with their start and end apart: 10, of which 9 were waited for; matrix products, arithmetic and copies ran while one was open for 5% of the time, Pallas kernels for 0%

commit v1 on v0

v1 whole, which is shorter than its diff:
```python
import functools

import jax
import jax.numpy as jnp
from jax import lax
from jax.experimental import pallas as pl
from jax.experimental.pallas import tpu as pltpu
from jax.sharding import PartitionSpec as P

LEVELS = 4
HALO = 16
WIDE = 256
MESH = pl.DeviceIdType.MESH
HIGHEST = lax.Precision.HIGHEST


def split2(x):
    high = x.astype(jnp.bfloat16).astype(jnp.float32)
    return high, x - high


def nt(a, b, precision=None):
    return lax.dot_general(a, b, (((1,), (1,)), ((), ())), precision=precision, preferred_element_type=jnp.float32)


def nn(a, b, precision=None):
    return lax.dot_general(a, b, (((1,), (0,)), ((), ())), precision=precision, preferred_element_type=jnp.float32)


def despike_block(xs, sp, y, ym1, c, frames):
    q = frames // 8

    def rows(i):
        return pl.ds(HALO + i, 8, stride=q)

    approx = [dict() for _ in range(LEVELS + 1)]
    plus = [dict() for _ in range(LEVELS + 1)]
    kept = [dict() for _ in range(LEVELS + 1)]
    flags = {}
    reco = [dict() for _ in range(LEVELS + 1)]
    first = [-1 - 15 + 2**j - 1 for j in range(LEVELS + 1)]
    last = [q - 1 + 15] * (LEVELS + 1)
    for i in range(first[0], last[0] + 1):
        approx[0][i] = xs[c, rows(i), :]
        if i >= -1:
            flags[i] = sp[c, rows(i), :]
        for j in range(1, LEVELS + 1):
            if i < first[j]:
                continue
            s = 2 ** (j - 1)
            here, lag = approx[j - 1][i], approx[j - 1][i - s]
            approx[j][i] = here + lag
            if -1 <= i <= q - 1 + (2**j - 1):
                detail = (here - lag) * (4.0 ** (LEVELS - j)) if j < LEVELS else here - lag
                kept[j][i] = jnp.where((flags[i] & s) == 0, detail, 0.0)
        t = i
        if t < -1:
            continue
        reco[LEVELS][t] = approx[LEVELS][t]
        for j in range(LEVELS, 0, -1):
            s = 2 ** (j - 1)
            if t > q - 1 + (2**j - 1):
                break
            plus[j][t] = reco[j][t] + kept[j][t]
            minus = reco[j][t] - kept[j][t]
            t = t - s
            if t < -1:
                break
            reco[j - 1][t] = plus[j][t] + minus
            if j == 1:
                value = reco[0][t] * (0.5 ** (2 * LEVELS))
                if t >= 0:
                    y[c, pl.ds(t, 8, stride=q), :] = value
                else:
                    ym1[:, pl.ds(pl.multiple_of(c * 128, 128), 128)] = value


def kernel(n_vox, n_tm, series, spikes, mt_ref, tissue_ref, y_out, cs_out, bs_out,
           xs, sp, y, ym1, yh, yl, mprev, own_m, in_rm, in_lm, out_rm, out_lm,
           own_s, in_rs, in_ls, out_rs, out_ls, sig, sig_in, gram, gram_in, wbuf, cmb, sacc,
           loc_sem, halo_send, halo_recv, mp_sem, rm_send, rm_recv, lm_send, lm_recv,
           rs_send, rs_recv, ls_send, ls_recv, sig_send, sig_recv, gr_send, gr_recv, y_sem):
    frames, cols = series.shape
    groups = cols // WIDE
    blocks = cols // 128
    p = lax.axis_index("tm")
    v = lax.axis_index("vox")
    right = lax.rem(p + 1, n_tm)
    left = lax.rem(p + n_tm - 1, n_tm)

    def at(g):
        return pl.ds(pl.multiple_of(g * WIDE, WIDE), WIDE)

    def lanes(c):
        return pl.ds(pl.multiple_of(c * 128, 128), 128)

    def local_copies(c):
        return (
            pltpu.make_async_copy(series.at[:, lanes(c)], xs.at[c, pl.ds(HALO, frames)], loc_sem.at[0, c]),
            pltpu.make_async_copy(spikes.at[:, lanes(c)], sp.at[c, pl.ds(HALO, frames)], loc_sem.at[1, c]),
        )

    def halo_copies(c):
        def copy(k, src, dst, target):
            return pltpu.make_async_remote_copy(
                src_ref=src, dst_ref=dst, send_sem=halo_send.at[k, c], recv_sem=halo_recv.at[k, c],
                device_id=(v, target), device_id_type=MESH)
        return (
            copy(0, series.at[pl.ds(frames - HALO, HALO), lanes(c)], xs.at[c, pl.ds(0, HALO)], right),
            copy(1, spikes.at[pl.ds(frames - 8, 8), lanes(c)], sp.at[c, pl.ds(HALO - 8, 8)], right),
            copy(2, series.at[pl.ds(0, HALO), lanes(c)], xs.at[c, pl.ds(HALO + frames, HALO)], left),
            copy(3, spikes.at[pl.ds(0, HALO), lanes(c)], sp.at[c, pl.ds(HALO + frames, HALO)], left),
        )

    @pl.loop(0, blocks)
    def _(c):
        for copy in local_copies(c):
            copy.start()

    barrier = pltpu.get_barrier_semaphore()
    for k in range(1, n_vox):
        pl.semaphore_signal(barrier, inc=1, device_id=(lax.rem(v + k, n_vox), p), device_id_type=MESH)
    for k in range(1, n_tm):
        pl.semaphore_signal(barrier, inc=1, device_id=(v, lax.rem(p + k, n_tm)), device_id_type=MESH)
    pl.semaphore_wait(barrier, n_vox - 1 + n_tm - 1)

    mp = pltpu.make_async_remote_copy(
        src_ref=mt_ref.at[:, pl.ds(frames - 128, 128)], dst_ref=mprev, send_sem=mp_sem.at[0], recv_sem=mp_sem.at[1],
        device_id=(v, right), device_id_type=MESH)
    mp.start()

    @pl.loop(0, blocks)
    def _(c):
        for copy in halo_copies(c):
            copy.start()

    @pl.when(p == 0)
    def _():
        in_rm[...] = jnp.zeros_like(in_rm)
        in_rs[...] = jnp.zeros_like(in_rs)

    @pl.when(p == n_tm - 1)
    def _():
        in_lm[...] = jnp.zeros_like(in_lm)
        in_ls[...] = jnp.zeros_like(in_ls)

    w = tissue_ref[...]
    w_high, w_low = split2(w)
    pad = jnp.zeros((5, cols), jnp.float32)
    wbuf[...] = jnp.concatenate([w_high, pad, w_low, pad], axis=0).astype(jnp.bfloat16)
    lane_at = lax.broadcasted_iota(jnp.int32, (8, frames), 1)
    later = jnp.where(p > 0, 1.0, 0.0).astype(jnp.float32)

    def derivative(base, before):
        return base - jnp.where(lane_at == 0, before * later, pltpu.roll(base, 1, 1))

    mp.wait()
    base = mt_ref[...]
    deriv = derivative(base, mprev[:, 127:128])
    conf_m = jnp.concatenate([base[:6], deriv[:6], (base * base)[:6], (deriv * deriv)[:6]], axis=0)
    cmb[...] = jnp.concatenate(split2(conf_m), axis=0).astype(jnp.bfloat16)
    sacc[...] = jnp.zeros_like(sacc)

    def scan_copy(src, dst, send, recv, r, target):
        return pltpu.make_async_remote_copy(
            src_ref=src.at[r], dst_ref=dst.at[r], send_sem=send.at[r], recv_sem=recv.at[r],
            device_id=(v, target), device_id_type=MESH)

    def forward(step, count, own, ins, outs, sends, recvs):
        for way, (first_at, end_at, target) in enumerate(((p, n_tm - 1, right), (n_tm - 1 - p, 0, left))):
            r = step - first_at

            @pl.when((r >= 0) & (r < count))
            def _():
                copy = scan_copy(outs[way], ins[way], sends[way], recvs[way], r, target)

                @pl.when(first_at > 0)
                def _():
                    copy.wait_recv()

                @pl.when(p != end_at)
                def _():
                    outs[way][r] = own[r] + ins[way][r]
                    copy.start()

    m_args = (own_m, (in_rm, in_lm), (out_rm, out_lm), (rm_send, lm_send), (rm_recv, lm_recv))
    s_args = (own_s, (in_rs, in_ls), (out_rs, out_ls), (rs_send, ls_send), (rs_recv, ls_recv))

    def y_copy(c):
        return pltpu.make_async_copy(y.at[c], y_out.at[:, lanes(c)], y_sem.at[c])

    @pl.loop(0, groups)
    def _(g):
        @pl.loop(0, 2)
        def _(k):
            c = 2 * g + k
            for copy in local_copies(c):
                copy.wait()
            for copy in halo_copies(c):
                copy.wait_recv()
            despike_block(xs, sp, y, ym1, c, frames)
            y_copy(c).start()

        block = jnp.concatenate([y[2 * g], y[2 * g + 1]], axis=1)
        high = block.astype(jnp.bfloat16)
        low = (block - high.astype(jnp.float32)).astype(jnp.bfloat16)
        yh[:, at(g)] = high
        yl[:, at(g)] = low
        wg = wbuf[:, at(g)]
        sacc[...] += nt(wg, high) + nt(wg, low)
        cross = nn(cmb[...], high) + nn(cmb[...], low)
        own_m[g] = cross[:24] + cross[24:]
        forward(g, groups, *m_args)

    sig[:, pl.ds(0, frames)] = sacc[0:8] + sacc[8:16]
    edge = jnp.sum(ym1[0:1] * tissue_ref[...], axis=1, keepdims=True)
    sig[0:3, pl.ds(frames, 128)] = jnp.broadcast_to(edge, (3, 128))
    sig[3:8, pl.ds(frames, 128)] = jnp.zeros((5, 128), jnp.float32)

    def sig_copy(k):
        return pltpu.make_async_remote_copy(
            src_ref=sig, dst_ref=sig_in.at[k], send_sem=sig_send.at[k], recv_sem=sig_recv.at[k],
            device_id=(lax.rem(v + k + 1, n_vox), p), device_id_type=MESH)

    for k in range(n_vox - 1):
        sig_copy(k).start()

    @pl.loop(groups, groups + n_tm - 1)
    def _(step):
        forward(step, groups, *m_args)

    total = sig[...]
    for k in range(n_vox - 1):
        sig_copy(k).wait()
        total = total + sig_in[k]
    total = total * (1.0 / float(cols * n_vox))
    base = total[:, :frames]
    deriv = derivative(base, total[:, frames:frames + 1])
    conf_s = jnp.concatenate(
        [base[:3], deriv[:3], (base * base)[:3], (deriv * deriv)[:3], jnp.zeros((4, frames), jnp.float32)], axis=0)
    csb = jnp.concatenate(split2(conf_s), axis=0).astype(jnp.bfloat16)
    base = mt_ref[...]
    deriv = derivative(base, mprev[:, 127:128])
    conf_m = jnp.concatenate([base[:6], deriv[:6], (base * base)[:6], (deriv * deriv)[:6]], axis=0)
    conf = jnp.concatenate([conf_m, conf_s], axis=0)
    gram[...] = nt(conf, jnp.concatenate([conf, jnp.zeros((88, frames), jnp.float32)], axis=0), HIGHEST)

    def gram_copy(k):
        return pltpu.make_async_remote_copy(
            src_ref=gram, dst_ref=gram_in.at[k], send_sem=gr_send.at[k], recv_sem=gr_recv.at[k],
            device_id=(v, lax.rem(p + k + 1, n_tm)), device_id_type=MESH)

    for k in range(n_tm - 1):
        gram_copy(k).start()

    for g in range(groups):
        part = pl.ds(g * WIDE, WIDE)
        cross = nn(csb, yh[:, part]) + nn(csb, yl[:, part])
        own_s[g] = cross[:16] + cross[16:]
        forward(g, groups, *s_args)

    conf48 = jnp.concatenate([conf, jnp.zeros((8, frames), jnp.float32)], axis=0)
    c_high, c_low = split2(conf48)
    cs_out[...] = jnp.concatenate([c_high, c_low, c_high], axis=0).astype(jnp.bfloat16)

    matrix = gram[...]
    for k in range(n_tm - 1):
        gram_copy(k).wait()
        matrix = matrix + gram_in[k]
    row_at = lax.broadcasted_iota(jnp.int32, (40, 128), 0)
    col_at = lax.broadcasted_iota(jnp.int32, (40, 128), 1)
    for k in range(36):
        pivot_row = matrix[k:k + 1, :]
        pivot_col = matrix[:, k:k + 1]
        inverse = 1.0 / pivot_row[:, k:k + 1]
        scaled = jnp.where(col_at[0:1] == k, inverse, pivot_row * inverse)
        rest = jnp.where(col_at == k, 0.0, matrix)
        matrix = jnp.where(row_at == k, scaled, rest - pivot_col * scaled)

    @pl.loop(groups, groups + n_tm - 1)
    def _(step):
        forward(step, groups, *s_args)

    inv = matrix[:, :40]
    for g in range(groups):
        cross = jnp.concatenate(
            [own_m[g] + in_rm[g] + in_lm[g], own_s[g] + in_rs[g] + in_ls[g]], axis=0)
        coef = nn(inv, cross, HIGHEST)
        b_high, b_low = split2(jnp.concatenate([coef, jnp.zeros((8, WIDE), jnp.float32)], axis=0))
        bs_out[:, pl.ds(g * WIDE, WIDE)] = jnp.concatenate([b_high, b_high, b_low], axis=0).astype(jnp.bfloat16)

    @pl.loop(0, groups)
    def _(g):
        for k in range(2):
            y_copy(2 * g + k).wait()
            for copy in halo_copies(2 * g + k):
                copy.wait_send()
        for args in (m_args, s_args):
            for way, (end_at, target) in enumerate(((n_tm - 1, right), (0, left))):
                @pl.when(p != end_at)
                def _():
                    scan_copy(args[2][way], args[1][way], args[3][way], args[4][way], g, target).wait_send()


def apply_kernel(y_ref, cs_ref, bs_ref, out_ref):
    out_ref[...] = y_ref[...] - lax.dot_general(
        cs_ref[...], bs_ref[...], (((0,), (0,)), ((), ())), preferred_element_type=jnp.float32)


def local(n_vox, n_tm, series, spikes, motion, tissue):
    frames, cols = series.shape
    groups = cols // WIDE
    blocks = cols // 128
    mt = jnp.pad(motion.T, ((0, 2), (0, 0)))
    f32, bf16 = jnp.float32, jnp.bfloat16
    vmem = pl.BlockSpec(memory_space=pltpu.VMEM)
    hbm = pl.BlockSpec(memory_space=pl.ANY)
    dma = pltpu.SemaphoreType.DMA
    sums_m = pltpu.VMEM((groups, 24, WIDE), f32)
    sums_s = pltpu.VMEM((groups, 16, WIDE), f32)
    y, cs, bs = pl.pallas_call(
        functools.partial(kernel, n_vox, n_tm),
        out_shape=(
            jax.ShapeDtypeStruct((frames, cols), f32),
            jax.ShapeDtypeStruct((144, frames), bf16),
            jax.ShapeDtypeStruct((144, cols), bf16),
        ),
        in_specs=[hbm, hbm, vmem, vmem],
        out_specs=[hbm, vmem, vmem],
        scratch_shapes=[
            pltpu.VMEM((blocks, frames + 2 * HALO, 128), f32),
            pltpu.VMEM((blocks, frames + 2 * HALO, 128), jnp.int32),
            pltpu.VMEM((blocks, frames, 128), f32),
            pltpu.VMEM((8, cols), f32),
            pltpu.VMEM((frames, cols), bf16),
            pltpu.VMEM((frames, cols), bf16),
            pltpu.VMEM((8, 128), f32),
            sums_m, sums_m, sums_m, sums_m, sums_m,
            sums_s, sums_s, sums_s, sums_s, sums_s,
            pltpu.VMEM((8, frames + 128), f32),
            pltpu.VMEM((n_vox - 1, 8, frames + 128), f32),
            pltpu.VMEM((40, 128), f32),
            pltpu.VMEM((n_tm - 1, 40, 128), f32),
            pltpu.VMEM((16, cols), bf16),
            pltpu.VMEM((48, frames), bf16),
            pltpu.VMEM((16, frames), f32),
            dma((2, blocks)), dma((4, blocks)), dma((4, blocks)), dma((2,)),
            dma((groups,)), dma((groups,)), dma((groups,)), dma((groups,)),
            dma((groups,)), dma((groups,)), dma((groups,)), dma((groups,)),
            dma((n_vox - 1,)), dma((n_vox - 1,)), dma((n_tm - 1,)), dma((n_tm - 1,)),
            dma((blocks,)),
        ],
        compiler_params=pltpu.CompilerParams(
            collective_id=0, has_side_effects=True, vmem_limit_bytes=48 * 1024 * 1024),
        cost_estimate=pl.CostEstimate(flops=10**9, bytes_accessed=12 * frames * cols, transcendentals=0),
        name="despike_and_fit",
    )(series, spikes, mt, tissue)
    return pl.pallas_call(
        apply_kernel,
        grid=(groups,),
        out_shape=jax.ShapeDtypeStruct((frames, cols), f32),
        in_specs=[
            pl.BlockSpec((frames, WIDE), lambda g: (0, g)),
            pl.BlockSpec((144, frames), lambda g: (0, 0)),
            pl.BlockSpec((144, WIDE), lambda g: (0, g)),
        ],
        out_specs=pl.BlockSpec((frames, WIDE), lambda g: (0, g)),
        compiler_params=pltpu.CompilerParams(vmem_limit_bytes=32 * 1024 * 1024),
        name="apply_coefficients",
    )(y, cs, bs)


def solution(mesh):
    return jax.shard_map(
        functools.partial(local, mesh.shape["vox"], mesh.shape["tm"]),
        mesh=mesh,
        in_specs=(P("tm", "vox"), P("tm", "vox"), P("tm", None), P(None, "vox")),
        out_specs=P("tm", "vox"),
        check_vma=False,
    )
```

time: 186 us -> 79.6 us (0.43)
  Pallas kernels: 0 us -> 77.8 us
  waiting for transfers between devices: 58.1 us -> 0 us
  other arithmetic: 38.5 us -> 0 us
  blocking collectives: 34.6 us -> 0 us
  matrix products: 17.8 us -> 0 us
  between operations: 13.8 us -> 0.01 us
  starting transfers between devices: 13.3 us -> 0 us
  local copies, waits for them, and re-layouts: 9.3 us -> 1.48 us
    pallas_call x0 -> x2, Pallas kernels: none -> 77.8 us  [the longest x1 72.9 us: local(): pl.pallas_call(functools.partial(kernel, n_vox, n_tm), out_shape=(jax.Sha...]
    psum x2 -> x0, blocking collectives: 34.6 us -> none  [the longest x1 22.6 us: local(): gram_matrix, cross_products = lax.psum((gram_matrix, cross_products), 'tm')]
    psum x1 -> x0, waiting for transfers between devices: 30.1 us -> none  [local(): gram_matrix, cross_products = lax.psum((gram_matrix, cross_products), 'tm')]
    ppermute x9 -> x0, waiting for transfers between devices: 28 us -> none  [the longest x8 26.6 us: from_behind(): return lax.ppermute(block, axis, route)]
    mul x5 -> x0, other arithmetic: 21.2 us -> none  [the longest x4 21.1 us: despike_levelwise(): kept_list.append(detail * keep_level(spikes, level))]
    dot_general x4 -> x0, matrix products: 15.9 us -> none  [precise_product(): jnp.dot(left, right, precision=lax.Precision.HIGHEST, preferred_element_t...]
    ppermute x9 -> x0, starting transfers between devices: 13.3 us -> none  [the longest x8 12 us: from_behind(): return lax.ppermute(block, axis, route)]
    add x4 -> x0, other arithmetic: 9.76 us -> none  [despike_levelwise(): approx = (approx + lead_approx) * 0.5 + (kept - lead_kept) * 0.5]
  transfers between devices with their start and end apart: 10 -> 0, of which waited for: 9 -> 0; matrix products, arithmetic and copies ran while one was open for 5% -> 0% of each run, Pallas kernels for 0% -> 0%
where the time goes in v1:
time: 79.6 us; the launch traced here: 79.3 us
  Pallas kernels  77.8 us (98%)
  local copies, waits for them, and re-layouts  1.48 us (2%)
    pallas_call x1, Pallas kernels, local(): pl.pallas_call(functools.partial(kernel, n_vox, n_tm), out_shape=(jax.Sha...  72.9 us
    pallas_call x1, Pallas kernels, local(): pl.pallas_call(apply_kernel, grid=(groups,), out_shape=jax.ShapeDtypeStru...  4.9 us

profile of v1, /device:TPU:0, one launch (start us, length us, event | category | flops | bytes accessed | tf_op | source)
XLA Modules:
  0.0 79.3 jit_solution(13082222366034145219)
XLA Ops:
  0.0 0.7 pad.4.mt_ref
  0.7 0.0 copy-start
  0.7 0.8 copy-done
  1.5 72.9 %despike_and_fit.1 = (f32[512,2048]{1,0:T(8,128)S(1)}, bf16[144,512]{1,0:T(8,128)(2,1)S(1)}, bf16[144,2048]{1,0:T(8,128)(2,1)S(1)}) custom-call(f32[512,2048]{1,0:T(8,128)} %series.1, s32[512,2048]{1,0:T(8,128)} %spikes.1, f32[8,512]{1,0:T(8,128)S(1)} %pad.4.mt_ref, f32[3,2048]{1,0:T(4,128)S(1)} %copy-done), custom_call_target="tpu_custom_call" | custom-call | flops 1000000000 | bytes 12582912 | tf_op jit(solution)/shard_map/despike_and_fit/pallas_call | solution.py:321
  74.4 4.9 %apply_coefficients.1 = f32[512,2048]{1,0:T(8,128)} custom-call(f32[512,2048]{1,0:T(8,128)S(1)} %get-tuple-element.8.y_ref, bf16[144,512]{1,0:T(8,128)(2,1)S(1)} %get-tuple-element.9.cs_ref, bf16[144,2048]{1,0:T(8,128)(2,1)S(1)} %get-tuple-element.10.bs_ref), custom_call_target="tpu_custom_call" | custom-call | tf_op jit(solution)/shard_map/apply_coefficients/pallas_call | solution.py:358
Async XLA Ops:
  0.7 0.8 copy-start

commit v2 on v1

--- a/solution.py
+++ b/solution.py
@@ -10,6 +10,9 @@
 LEVELS = 4
 HALO = 16
 WIDE = 256
+LAG_M = 4
+LAG_S = 4
+APPLY = 512
 MESH = pl.DeviceIdType.MESH
 HIGHEST = lax.Precision.HIGHEST
 
@@ -166,9 +169,9 @@
             src_ref=src.at[r], dst_ref=dst.at[r], send_sem=send.at[r], recv_sem=recv.at[r],
             device_id=(v, target), device_id_type=MESH)
 
-    def forward(step, count, own, ins, outs, sends, recvs):
+    def forward(step, lag, count, own, ins, outs, sends, recvs):
         for way, (first_at, end_at, target) in enumerate(((p, n_tm - 1, right), (n_tm - 1 - p, 0, left))):
-            r = step - first_at
+            r = step - lag * first_at
 
             @pl.when((r >= 0) & (r < count))
             def _():
@@ -210,12 +213,15 @@
         sacc[...] += nt(wg, high) + nt(wg, low)
         cross = nn(cmb[...], high) + nn(cmb[...], low)
         own_m[g] = cross[:24] + cross[24:]
-        forward(g, groups, *m_args)
-
-    sig[:, pl.ds(0, frames)] = sacc[0:8] + sacc[8:16]
+        forward(g, LAG_M, groups, *m_args)
+
+    parts = sacc[0:8] + sacc[8:16]
     edge = jnp.sum(ym1[0:1] * tissue_ref[...], axis=1, keepdims=True)
-    sig[0:3, pl.ds(frames, 128)] = jnp.broadcast_to(edge, (3, 128))
-    sig[3:8, pl.ds(frames, 128)] = jnp.zeros((5, 128), jnp.float32)
+    pieces = [parts[0:3, 128 * b:128 * b + 128] for b in range(frames // 128)] + [jnp.broadcast_to(edge, (3, 128))]
+    unused = sig.shape[0] - 3 * len(pieces)
+    if unused:
+        pieces.append(jnp.zeros((unused, 128), jnp.float32))
+    sig[...] = jnp.concatenate(pieces, axis=0)
 
     def sig_copy(k):
         return pltpu.make_async_remote_copy(
@@ -225,17 +231,22 @@
     for k in range(n_vox - 1):
         sig_copy(k).start()
 
-    @pl.loop(groups, groups + n_tm - 1)
-    def _(step):
-        forward(step, groups, *m_args)
+    steps_m = groups + LAG_M * (n_tm - 1)
+    steps_s = groups + LAG_S * (n_tm - 1)
+    early = min(groups + 2, steps_m)
+    for step in range(groups, early):
+        forward(step, LAG_M, groups, *m_args)
 
     total = sig[...]
     for k in range(n_vox - 1):
         sig_copy(k).wait()
         total = total + sig_in[k]
     total = total * (1.0 / float(cols * n_vox))
-    base = total[:, :frames]
-    deriv = derivative(base, total[:, frames:frames + 1])
+    nb = frames // 128
+    base = jnp.concatenate([total[3 * b:3 * b + 3] for b in range(nb)], axis=1)
+    base = jnp.concatenate([base, jnp.zeros((5, frames), jnp.float32)], axis=0)
+    before = jnp.concatenate([total[3 * nb:3 * nb + 3, 0:1], jnp.zeros((5, 1), jnp.float32)], axis=0)
+    deriv = derivative(base, before)
     conf_s = jnp.concatenate(
         [base[:3], deriv[:3], (base * base)[:3], (deriv * deriv)[:3], jnp.zeros((4, frames), jnp.float32)], axis=0)
     csb = jnp.concatenate(split2(conf_s), axis=0).astype(jnp.bfloat16)
@@ -253,33 +264,44 @@
     for k in range(n_tm - 1):
         gram_copy(k).start()
 
-    for g in range(groups):
-        part = pl.ds(g * WIDE, WIDE)
-        cross = nn(csb, yh[:, part]) + nn(csb, yl[:, part])
-        own_s[g] = cross[:16] + cross[16:]
-        forward(g, groups, *s_args)
-
-    conf48 = jnp.concatenate([conf, jnp.zeros((8, frames), jnp.float32)], axis=0)
-    c_high, c_low = split2(conf48)
-    cs_out[...] = jnp.concatenate([c_high, c_low, c_high], axis=0).astype(jnp.bfloat16)
-
-    matrix = gram[...]
-    for k in range(n_tm - 1):
-        gram_copy(k).wait()
-        matrix = matrix + gram_in[k]
     row_at = lax.broadcasted_iota(jnp.int32, (40, 128), 0)
     col_at = lax.broadcasted_iota(jnp.int32, (40, 128), 1)
-    for k in range(36):
+
+    def eliminate(matrix, k):
         pivot_row = matrix[k:k + 1, :]
         pivot_col = matrix[:, k:k + 1]
         inverse = 1.0 / pivot_row[:, k:k + 1]
         scaled = jnp.where(col_at[0:1] == k, inverse, pivot_row * inverse)
         rest = jnp.where(col_at == k, 0.0, matrix)
-        matrix = jnp.where(row_at == k, scaled, rest - pivot_col * scaled)
-
-    @pl.loop(groups, groups + n_tm - 1)
-    def _(step):
-        forward(step, groups, *s_args)
+        return jnp.where(row_at == k, scaled, rest - pivot_col * scaled)
+
+    matrix = None
+    done = 0
+    gram_at = LAG_S
+    for step in range(max(steps_s, steps_m - early)):
+        if step < groups:
+            part = pl.ds(step * WIDE, WIDE)
+            cross = nn(csb, yh[:, part]) + nn(csb, yl[:, part])
+            own_s[step] = cross[:16] + cross[16:]
+        if step < steps_s:
+            forward(step, LAG_S, groups, *s_args)
+        if early + step < steps_m:
+            forward(early + step, LAG_M, groups, *m_args)
+        if step == gram_at:
+            matrix = gram[...]
+            for k in range(n_tm - 1):
+                gram_copy(k).wait()
+                matrix = matrix + gram_in[k]
+        if step >= gram_at:
+            for k in range(done, min(done + 3, 36)):
+                matrix = eliminate(matrix, k)
+            done = min(done + 3, 36)
+        if step == gram_at - 1:
+            conf48 = jnp.concatenate([conf, jnp.zeros((8, frames), jnp.float32)], axis=0)
+            c_high, c_low = split2(conf48)
+            cs_out[...] = jnp.transpose(jnp.concatenate([c_high, c_low, c_high], axis=0)).astype(jnp.bfloat16)
+    for k in range(done, 36):
+        matrix = eliminate(matrix, k)
 
     inv = matrix[:, :40]
     for g in range(groups):
@@ -303,14 +325,15 @@
 
 
 def apply_kernel(y_ref, cs_ref, bs_ref, out_ref):
-    out_ref[...] = y_ref[...] - lax.dot_general(
-        cs_ref[...], bs_ref[...], (((0,), (0,)), ((), ())), preferred_element_type=jnp.float32)
+    at = pl.ds(pl.multiple_of(pl.program_id(0) * APPLY, APPLY), APPLY)
+    out_ref[...] = y_ref[:, at] - nn(cs_ref[...], bs_ref[:, at])
 
 
 def local(n_vox, n_tm, series, spikes, motion, tissue):
     frames, cols = series.shape
     groups = cols // WIDE
     blocks = cols // 128
+    packed = -(-3 * (frames // 128 + 1) // 8) * 8
     mt = jnp.pad(motion.T, ((0, 2), (0, 0)))
     f32, bf16 = jnp.float32, jnp.bfloat16
     vmem = pl.BlockSpec(memory_space=pltpu.VMEM)
@@ -322,7 +345,7 @@
         functools.partial(kernel, n_vox, n_tm),
         out_shape=(
             jax.ShapeDtypeStruct((frames, cols), f32),
-            jax.ShapeDtypeStruct((144, frames), bf16),
+            jax.ShapeDtypeStruct((frames, 144), bf16),
             jax.ShapeDtypeStruct((144, cols), bf16),
         ),
         in_specs=[hbm, hbm, vmem, vmem],
@@ -337,8 +360,8 @@
             pltpu.VMEM((8, 128), f32),
             sums_m, sums_m, sums_m, sums_m, sums_m,
             sums_s, sums_s, sums_s, sums_s, sums_s,
-            pltpu.VMEM((8, frames + 128), f32),
-            pltpu.VMEM((n_vox - 1, 8, frames + 128), f32),
+            pltpu.VMEM((packed, 128), f32),
+            pltpu.VMEM((n_vox - 1, packed, 128), f32),
             pltpu.VMEM((40, 128), f32),
             pltpu.VMEM((n_tm - 1, 40, 128), f32),
             pltpu.VMEM((16, cols), bf16),
@@ -357,14 +380,10 @@
     )(series, spikes, mt, tissue)
     return pl.pallas_call(
         apply_kernel,
-        grid=(groups,),
+        grid=(cols // APPLY,),
         out_shape=jax.ShapeDtypeStruct((frames, cols), f32),
-        in_specs=[
-            pl.BlockSpec((frames, WIDE), lambda g: (0, g)),
-            pl.BlockSpec((144, frames), lambda g: (0, 0)),
-            pl.BlockSpec((144, WIDE), lambda g: (0, g)),
-        ],
-        out_specs=pl.BlockSpec((frames, WIDE), lambda g: (0, g)),
+        in_specs=[vmem, vmem, vmem],
+        out_specs=pl.BlockSpec((frames, APPLY), lambda g: (0, g)),
         compiler_params=pltpu.CompilerParams(vmem_limit_bytes=32 * 1024 * 1024),
         name="apply_coefficients",
     )(y, cs, bs)

time: 79.6 us -> 50.5 us (0.63)
  Pallas kernels: 77.8 us -> 48.7 us
    pallas_call x1, Pallas kernels: 72.9 us -> 45.9 us  [local(): pl.pallas_call(functools.partial(kernel, n_vox, n_tm), out_shape=(jax.Sha...]
    pallas_call x1, Pallas kernels: 4.9 us -> 2.88 us  [local(): pl.pallas_call(apply_kernel, grid=(cols // APPLY,), out_shape=jax.ShapeDt...]
where the time goes in v2:
time: 50.5 us; the launch traced here: 50.2 us
  Pallas kernels  48.7 us (96%)
  local copies, waits for them, and re-layouts  1.48 us (3%)
    pallas_call x1, Pallas kernels, local(): pl.pallas_call(functools.partial(kernel, n_vox, n_tm), out_shape=(jax.Sha...  45.9 us
    pallas_call x1, Pallas kernels, local(): pl.pallas_call(apply_kernel, grid=(cols // APPLY,), out_shape=jax.ShapeDt...  2.88 us

profile of v2, /device:TPU:0, one launch (start us, length us, event | category | flops | bytes accessed | tf_op | source)
XLA Modules:
  0.0 50.2 jit_solution(7827910743171848773)
XLA Ops:
  0.0 0.7 %pad.4.mt_ref = f32[8,512]{1,0:T(8,128)S(1)} pad(f32[6,512]{1,0:T(8,128)} %bitcast.1, f32[]{:T(128)} %constant.2.clone.1), padding=0_2x0_0 | pad | bytes 28676 | tf_op jit(solution)/shard_map/jit(_pad)/pad | solution.py:337
  0.7 0.0 copy-start
  0.7 0.8 %copy-done = f32[3,2048]{1,0:T(4,128)S(1)} copy-done((f32[3,2048]{1,0:T(4,128)S(1)}, f32[3,2048]{1,0:T(4,128)}, u32[]{:S(2)}) %copy-start) | copy-done | bytes 24600
  1.5 45.9 %despike_and_fit.1 = (f32[512,2048]{1,0:T(8,128)S(1)}, bf16[512,144]{1,0:T(8,128)(2,1)S(1)}, bf16[144,2048]{1,0:T(8,128)(2,1)S(1)}) custom-call(f32[512,2048]{1,0:T(8,128)} %series.1, s32[512,2048]{1,0:T(8,128)} %spikes.1, f32[8,512]{1,0:T(8,128)S(1)} %pad.4.mt_ref, f32[3,2048]{1,0:T(4,128)S(1)} %copy-done), custom_call_target="tpu_custom_call" | custom-call | flops 1000000000 | bytes 12582912 | tf_op jit(solution)/shard_map/despike_and_fit/pallas_call | solution.py:344
  47.3 2.9 %apply_coefficients.1 = f32[512,2048]{1,0:T(8,128)} custom-call(f32[512,2048]{1,0:T(8,128)S(1)} %get-tuple-element.8.y_ref, bf16[512,144]{1,0:T(8,128)(2,1)S(1)} %get-tuple-element.9.cs_ref, bf16[144,2048]{1,0:T(8,128)(2,1)S(1)} %get-tuple-element.10.bs_ref), custom_call_target="tpu_custom_call" | custom-call | tf_op jit(solution)/shard_map/apply_coefficients/pallas_call | solution.py:381
Async XLA Ops:
  0.7 0.8 %copy-start = (f32[3,2048]{1,0:T(4,128)S(1)}, f32[3,2048]{1,0:T(4,128)}, u32[]{:S(2)}) copy-start(f32[3,2048]{1,0:T(4,128)} %tissue_ref.1) | copy-start | bytes 73732
